TPU v7x, 32 devices: a whole 2x2x4 slice. The times are simulated.
32 devices in a mesh: occ: 32 (over z, y, x, core).
Axes of the slice: x: 2, y: 2, z: 4, core: 2. Of those that a mesh axis runs over, the one named last changes fastest.
Arguments:
- ri_factors: bfloat16 [32, 512, 1536], P('occ'), may hold values from -1.09375 to 1.09375
- occ_energy: float32 [32], P('occ'), may hold values from -1.5 to -0.3
- vir_energy: float32 [512], replicated, may hold values from 0.2 to 2.5
- partner: int32 [2, 32], P(None, 'occ'), may hold values from 0 to 31, as said below
- pair_weight: int32 [2, 32], P(None, 'occ'), may hold values from 1 to 2, as said below
Outputs:
- response: float32 [32, 512, 1536], P('occ')
- aux_density: float32 [1536, 1536], P('occ')
Inputs may be any that keep to these rules, and one draw needn't show every extreme that they name: In each round the partner of orbital i is i XOR m for one nonzero m of that round, so partners pair up and the pair list is symmetric; in the first round m = 16. `pair_weight`: the two orbitals of a pair carry the same weight in a round.
All inputs are finite; a program needn't handle non-finite values.
Results may differ from a plain program's by a relative error of at most 0.0036.
Values may be sent and summed in bfloat16 or wider, within the bound.
A program may use at most 64 MiB of HBM per device.

v0:
```python
import jax
import jax.numpy as jnp
from jax import lax
from jax.sharding import PartitionSpec as P

ROUNDS = 2


def from_partner(value, axis, apart):
    mask = 2**apart
    pairs = [(source, source ^ mask) for source in range(lax.axis_size(axis))]
    return lax.ppermute(value, axis, pairs)


def density_rows(response_parts, own_block, row_count):
    accumulated = jnp.zeros((row_count, own_block.shape[1]), jnp.float32)
    for response_part in response_parts:
        accumulated = lax.dot_general(
            response_part, own_block, (((0,), (0,)), ((), ())), preferred_element_type=jnp.float32
        )
    return accumulated


def route_section(block, bit_pos):
    return from_partner(block, "occ", bit_pos)


def body(ri_factors, occ_energy, vir_energy, partner, pair_weight):
    own_block = ri_factors[0]
    devices = lax.axis_size("occ")
    my_index = lax.axis_index("occ")
    energies = lax.all_gather(occ_energy, "occ", axis=0, tiled=True)
    positions = lax.iota(jnp.int32, devices)
    sections = devices.bit_length() - 1
    share_rows = own_block.shape[1] // devices
    response_list = []
    for round_num in range(ROUNDS):
        other = partner[round_num, 0]
        xor_mask = jnp.bitwise_xor(other, my_index)
        fetched = own_block
        for bit_pos in range(sections):
            taking = jnp.bitwise_and(jnp.right_shift(xor_mask, bit_pos), 1) == 1
            fetched = lax.cond(
                taking,
                lambda block, section_bit=bit_pos: route_section(block, section_bit),
                lambda block: block,
                fetched,
            )
        partner_energy = jnp.sum(jnp.where(positions == other, energies, 0.0))
        coulomb = lax.dot_general(
            own_block, fetched, (((1,), (1,)), ((), ())), preferred_element_type=jnp.float32
        )
        denominator = occ_energy[0] + partner_energy - vir_energy[:, None] - vir_energy[None, :]
        amplitudes = coulomb / denominator
        combined = (2.0 * amplitudes - amplitudes.T).astype(jnp.bfloat16)
        weight_now = pair_weight[round_num, 0].astype(jnp.float32)
        response_part = (
            weight_now * jnp.dot(combined, fetched, preferred_element_type=jnp.float32)
        ).astype(jnp.bfloat16)
        response_list.append(response_part)
    density = jnp.zeros((share_rows, own_block.shape[1]), jnp.float32)
    for response_part in response_list:
        density = density + lax.psum_scatter(
            density_rows((response_part,), own_block, share_rows * lax.axis_size("occ")),
            "occ",
            scatter_dimension=0,
            tiled=True,
        )
    summed = jnp.zeros(own_block.shape, jnp.float32)
    for response_part in response_list:
        summed = summed + response_part.astype(jnp.float32)
    return (summed[None], density / float(devices))


def solution(mesh):
    placed = (P("occ", None, None), P("occ"), P(), P(None, "occ"), P(None, "occ"))
    return jax.shard_map(
        body,
        mesh=mesh,
        in_specs=placed,
        out_specs=(P("occ", None, None), P("occ", None)),
        check_vma=False,
    )
```

profile of v0, /device:TPU:0, one launch (start us, length us, event | category | flops | bytes accessed | tf_op | source)
XLA Modules:
  0.0 372.9 jit_solution(6853990797525979405)
XLA Ops:
  7.2 0.0 reduce-scatter.2.cloned.1.call-start
  7.2 1.3 fusion.32
  10.5 0.1 dynamic-update-slice
  10.6 42.0 %all-reduce = f32[32]{0:T(128)S(1)} all-reduce(f32[32]{0:T(128)S(1)} %dynamic-update-slice), channel_id=1, replica_groups=mesh['occ'=32] {'occ'}, use_global_device_ids=true, to_apply=%add | all-reduce | flops 32 | bytes 256
  52.6 2.0 fusion.20
  54.5 1.3 fusion.31
  57.1 2.7 conditional.10
  57.2 2.7 copy.20
  59.8 0.0 copy-start
  59.8 71.3 %conditional.14 = (bf16[512,1536]{1,0:T(8,128)(2,1)}) conditional(s32[]{:T(128)} %convert_element_type.62, bf16[512,1536]{1,0:T(8,128)(2,1)} %get-tuple-element.63, bf16[512,1536]{1,0:T(8,128)(2,1)} %get-tuple-element.63), branch_computations={%region_8.0_spmd, %region_9.0_spmd} | conditional | bytes 9437232 | solution.py:43
  59.8 2.3 collective-permute-start.4
  62.2 67.8 %collective-permute-done.4 = bf16[512,1536]{1,0:T(8,128)(2,1)S(1)} collective-permute-done((bf16[512,1536]{1,0:T(8,128)(2,1)}, bf16[512,1536]{1,0:T(8,128)(2,1)S(1)}, u32[]{:S(2)}, u32[]{:S(2)}) %collective-permute-start.4) | collective-permute-done | bytes 1572896 | tf_op jit(solution)/shard_map/cond/branch_1_fun/ppermute | solution.py:12
  130.0 1.2 copy.29
  131.2 0.0 copy-done
  131.2 2.4 fusion.27
  133.6 1.3 copy.7
  134.9 1.1 conditional.15
  134.9 1.1 copy.9
  136.0 36.6 %conditional.16 = (bf16[512,1536]{1,0:T(8,128)(2,1)}) conditional(s32[]{:T(128)} %convert_element_type.75, bf16[512,1536]{1,0:T(8,128)(2,1)} %get-tuple-element.65, bf16[512,1536]{1,0:T(8,128)(2,1)} %get-tuple-element.65), branch_computations={%region_13.14_spmd, %region_14.15_spmd} | conditional | bytes 9437232 | solution.py:43
  136.0 1.3 collective-permute-start.6
  137.4 34.2 %collective-permute-done.6 = bf16[512,1536]{1,0:T(8,128)(2,1)S(1)} collective-permute-done((bf16[512,1536]{1,0:T(8,128)(2,1)}, bf16[512,1536]{1,0:T(8,128)(2,1)S(1)}, u32[]{:S(2)}, u32[]{:S(2)}) %collective-permute-start.6) | collective-permute-done | bytes 1572896 | tf_op jit(solution)/shard_map/cond/branch_1_fun/ppermute | solution.py:12
  171.5 1.1 copy.12
  172.7 35.7 %conditional.18 = (bf16[512,1536]{1,0:T(8,128)(2,1)}) conditional(s32[]{:T(128)} %convert_element_type.73, bf16[512,1536]{1,0:T(8,128)(2,1)} %get-tuple-element.67, bf16[512,1536]{1,0:T(8,128)(2,1)} %get-tuple-element.67), branch_computations={%region_17.18_spmd, %region_18.19_spmd} | conditional | bytes 9437232 | solution.py:43
  172.7 0.0 collective-permute-start.8
  172.7 34.6 %collective-permute-done.8 = bf16[512,1536]{1,0:T(8,128)(2,1)S(1)} collective-permute-done((bf16[512,1536]{1,0:T(8,128)(2,1)}, bf16[512,1536]{1,0:T(8,128)(2,1)S(1)}, u32[]{:S(2)}, u32[]{:S(2)}) %collective-permute-start.8) | collective-permute-done | bytes 1572896 | tf_op jit(solution)/shard_map/cond/branch_1_fun/ppermute | solution.py:12
  207.3 1.1 copy.16
  208.4 3.4 fusion.25
  211.8 0.0 copy-start.5
  211.8 2.5 copy.8
  215.6 0.0 copy-done.5
  215.6 2.8 fusion
  218.5 0.0 copy-start.1
  218.5 0.0 copy-start.3
  218.5 0.0 copy-start.4
  218.5 2.7 fusion.23
  221.2 0.0 copy-done.1
  221.2 0.0 copy-done.3
  221.2 0.0 copy-done.4
  221.2 2.6 fusion.1
  223.8 5.4 %convolution_add_fusion = f32[1536,1536]{1,0:T(8,128)} fusion(f32[1536,1536]{1,0:T(8,128)S(1)} %fusion.23, bf16[512,1536]{1,0:T(8,128)(2,1)S(1)} %fusion.1, bf16[1,512,1536]{2,1,0:T(8,128)(2,1)S(1)} %copy-done), kind=kOutput, calls=%fused_computation | convolution fusion | flops 2418278400 | bytes 22020096 | tf_op jit(solution)/shard_map/dot_general | solution.py:18
  229.1 0.0 copy-start.2
  229.1 0.0 reduce-scatter.2.cloned.1.call-update
  229.2 1.4 copy-done.2
  230.5 2.1 add_bitcast_fusion
  232.7 131.7 %reduce-scatter.2.cloned.1.call-done = f32[48,1536]{1,0:T(8,128)} async-done(((f32[1536,1536]{1,0:T(8,128)}), f32[48,1536]{1,0:T(8,128)}) %reduce-scatter.2.cloned.1.call-update) | async-done | bytes 294928 | tf_op jit(solution)/shard_map/reduce_scatter | solution.py:63
  364.3 1.7 broadcast_multiply_fusion
  (7 shorter events, 0.0 us)
Async XLA Ops:
  7.2 357.1 %reduce-scatter.2.cloned.1.call-start = ((), (), s32[]{:S(2)}) async-start(), calls=%async_computation.1 | async-start | bytes 9732096 | tf_op jit(solution)/shard_map/reduce_scatter | solution.py:63
  59.8 71.3 %copy-start = (bf16[1,512,1536]{2,1,0:T(8,128)(2,1)S(1)}, bf16[1,512,1536]{2,1,0:T(8,128)(2,1)}, u32[]{:S(2)}) copy-start(bf16[1,512,1536]{2,1,0:T(8,128)(2,1)} %param.25) | copy-start | bytes 4718596
  59.8 70.1 %collective-permute-start.4 = (bf16[512,1536]{1,0:T(8,128)(2,1)}, bf16[512,1536]{1,0:T(8,128)(2,1)S(1)}, u32[]{:S(2)}, u32[]{:S(2)}) collective-permute-start(bf16[512,1536]{1,0:T(8,128)(2,1)} %param.9), channel_id=1, source_target_pairs={{0,16},{1,17},{2,18},{3,19},{4,20},{5,21},{6,22},{7,23},{8,24},{9,... | collective-permute-start | bytes 4718600 | tf_op jit(solution)/shard_map/cond/branch_1_fun/ppermute | solution.py:12
  136.0 35.5 %collective-permute-start.6 = (bf16[512,1536]{1,0:T(8,128)(2,1)}, bf16[512,1536]{1,0:T(8,128)(2,1)S(1)}, u32[]{:S(2)}, u32[]{:S(2)}) collective-permute-start(bf16[512,1536]{1,0:T(8,128)(2,1)} %param.13), channel_id=1, source_target_pairs={{0,2},{1,3},{2,0},{3,1},{4,6},{5,7},{6,4},{7,5},{8,10},{9,11},{10,... | collective-permute-start | bytes 4718600 | tf_op jit(solution)/shard_map/cond/branch_1_fun/ppermute | solution.py:12
  172.7 34.6 %collective-permute-start.8 = (bf16[512,1536]{1,0:T(8,128)(2,1)}, bf16[512,1536]{1,0:T(8,128)(2,1)S(1)}, u32[]{:S(2)}, u32[]{:S(2)}) collective-permute-start(bf16[512,1536]{1,0:T(8,128)(2,1)} %param.17), channel_id=1, source_target_pairs={{0,8},{1,9},{2,10},{3,11},{4,12},{5,13},{6,14},{7,15},{8,0},{9,1},... | collective-permute-start | bytes 4718600 | tf_op jit(solution)/shard_map/cond/branch_1_fun/ppermute | solution.py:12
  211.8 3.8 %copy-start.5 = (f32[512]{0:T(512)S(1)}, f32[512]{0:T(512)}, u32[]{:S(2)}) copy-start(f32[512]{0:T(512)} %param.27) | copy-start | bytes 6148
  218.5 2.7 copy-start.1
  218.5 2.7 copy-start.3
  218.5 2.7 copy-start.4
  229.1 1.4 copy-start.2
Sparse Core Ops, SparseCore 0:
  229.3 134.9 reduce-scatter.1
where the time goes:
time: 376 us; the launch traced here: 373 us
  waiting for transfers between devices  268 us (71%)
  blocking collectives  42 us (11%)
  matrix products  19.2 us (5%)
  between operations  18.6 us (5%)
  local copies, waits for them, and re-layouts  15.2 us (4%)
  other arithmetic  5.78 us (2%)
    ppermute x3, waiting for transfers between devices, from_partner(): return lax.ppermute(value, axis, pairs)  137 us
    reduce_scatter x1, waiting for transfers between devices, body(): lax.psum_scatter(density_rows((response_part,), own_block, share_rows * l...  132 us
    unnamed x1, blocking collectives  42 us
    dot_general x2, matrix products, density_rows(): lax.dot_general(response_part, own_block, (((0,), (0,)), ((), ())), prefe...  8.04 us
  transfers between devices with their start and end apart: 4, of which 4 were waited for; matrix products, arithmetic and copies ran while one was open for 1% of the time, Pallas kernels for 0%

commit v1 on v0

v1 whole, which is shorter than its diff:
```python
import functools

import jax
import jax.numpy as jnp
from jax import lax
from jax.experimental import pallas as pl
from jax.experimental.pallas import tpu as pltpu
from jax.sharding import PartitionSpec as P

ROUNDS = 2
AXIS = "occ"
CHAINS = 3
PIECES = 8


def chain_orders(bits):
    middle = list(range(1, bits - 1))
    orders = []
    for chain in range(CHAINS):
        turn = chain % max(len(middle), 1)
        orders.append([0] + middle[turn:] + middle[:turn] + ([bits - 1] if bits > 1 else []))
    return orders


def block_index(me, k, done, free):
    index = 0
    for bit in done:
        index = index + ((me // 2**bit) % 2) * 2**bit
    for place, bit in enumerate(free):
        index = index + ((k // 2**place) % 2) * 2**bit
    return index


def scatter_kernel(bits, orders, width, *refs):
    part_ref, out_ref, acc = refs[0], refs[1], refs[2]
    sends = refs[3 : 3 + bits]
    recvs = refs[3 + bits : 3 + 2 * bits]
    send_sem, recv_sem = refs[3 + 2 * bits], refs[4 + 2 * bits]
    me = lax.axis_index(AXIS)

    def peer(bit):
        own = (me // 2**bit) % 2
        return me + (1 - 2 * own) * 2**bit

    barrier = pltpu.get_barrier_semaphore()
    for bit in range(bits):
        pl.semaphore_signal(
            barrier, inc=1, device_id=(peer(bit),), device_id_type=pl.DeviceIdType.MESH
        )
    pl.semaphore_wait(barrier, bits)

    def copy(stage, chain):
        return pltpu.make_async_remote_copy(
            src_ref=sends[stage].at[chain],
            dst_ref=recvs[stage].at[chain],
            send_sem=send_sem.at[stage, chain],
            recv_sem=recv_sem.at[stage, chain],
            device_id=(peer(orders[chain][stage]),),
            device_id_type=pl.DeviceIdType.MESH,
        )

    def advance(stage, chain):
        order = orders[chain]
        bit = order[stage]
        before, free = order[:stage], order[stage + 1 :]
        columns = pl.ds(chain * width, width)
        count = 2 ** (bits - stage - 1)

        def arrived(side, k):
            return recvs[stage - 1][chain, side + 2 * k].astype(jnp.float32)

        def base(k, side):
            index = block_index(me, k, before, free) + side * 2**bit
            if stage == 0:
                return index, part_ref[index, :, columns]
            value = acc[index, :, columns] if stage > 1 else part_ref[index, :, columns]
            return index, value + arrived(side, k)

        mine = (me // 2**bit) % 2

        def send_one(k, _):
            index, value = base(k, 1 - mine)
            sends[stage][chain, k] = value.astype(jnp.bfloat16)
            return 0

        lax.fori_loop(0, count, send_one, 0)
        copy(stage, chain).start()
        if stage == 0:
            return

        def keep_one(k, _):
            index, value = base(k, mine)
            acc[index, :, columns] = value
            return 0

        lax.fori_loop(0, count, keep_one, 0)

    for chain in range(CHAINS):
        advance(0, chain)
    for stage in range(1, bits):
        for chain in range(CHAINS):
            copy(stage - 1, chain).wait()
            advance(stage, chain)
    for chain in range(CHAINS):
        columns = pl.ds(chain * width, width)
        copy(bits - 1, chain).wait()
        last = acc[me, :, columns] if bits > 1 else part_ref[me, :, columns]
        out_ref[:, columns] = last + recvs[bits - 1][chain, 0].astype(jnp.float32)


def density_scatter(partial):
    devices, rows, wide = partial.shape
    bits = devices.bit_length() - 1
    width = wide // CHAINS
    orders = chain_orders(bits)
    slots = [
        pltpu.VMEM((CHAINS, 2 ** (bits - stage - 1), rows, width), jnp.bfloat16)
        for stage in range(bits)
    ]
    return pl.pallas_call(
        functools.partial(scatter_kernel, bits, orders, width),
        out_shape=jax.ShapeDtypeStruct((rows, wide), jnp.float32),
        in_specs=[pl.BlockSpec(memory_space=pltpu.VMEM)],
        out_specs=pl.BlockSpec(memory_space=pltpu.VMEM),
        scratch_shapes=[pltpu.VMEM((devices, rows, wide), jnp.float32)]
        + slots
        + slots
        + [pltpu.SemaphoreType.DMA((bits, CHAINS)), pltpu.SemaphoreType.DMA((bits, CHAINS))],
        compiler_params=pltpu.CompilerParams(
            collective_id=0, has_side_effects=True, vmem_limit_bytes=58 * 2**20
        ),
    )(partial)


def exchange_kernel(bits, pieces, *refs):
    flags, own, energy, out0, out1, energies = refs[:6]
    stages = bits - 1
    held, arrived, held_e, arrived_e = refs[6:10]
    top_send, top_recv, low_send, low_recv = refs[10:14]
    me = lax.axis_index(AXIS)
    order = list(range(stages - 1, -1, -1))

    def peer(bit):
        mine = (me // 2**bit) % 2
        return me + (1 - 2 * mine) * 2**bit

    barrier = pltpu.get_barrier_semaphore()
    for bit in range(bits):
        pl.semaphore_signal(
            barrier, inc=1, device_id=(peer(bit),), device_id_type=pl.DeviceIdType.MESH
        )
    pl.semaphore_wait(barrier, bits)

    def remote(src, dst, send_sem, recv_sem, bit):
        return pltpu.make_async_remote_copy(
            src_ref=src,
            dst_ref=dst,
            send_sem=send_sem,
            recv_sem=recv_sem,
            device_id=(peer(bit),),
            device_id_type=pl.DeviceIdType.MESH,
        )

    def top(n):
        if n == pieces:
            src, dst = energy, energies.at[0]
        else:
            src, dst = own.at[n], out0.at[n]
        return remote(src, dst, top_send.at[n], top_recv.at[n], bits - 1)

    def lower(stage, n):
        if n == pieces:
            src, dst = held_e.at[stage], arrived_e.at[stage]
        else:
            src, dst = held.at[stage, n], arrived.at[stage, n]
        return remote(src, dst, low_send.at[stage, n], low_recv.at[stage, n], order[stage])

    def place(stage, n, value):
        if n == pieces:
            if stage == stages:
                energies[1] = value
            else:
                held_e[stage] = value
        elif stage == stages:
            out1[n] = value
        else:
            held[stage, n] = value
        if stage < stages:
            lower(stage, n).start()

    def enter(n):
        top(n).wait()
        taking = flags[bits - 1] == 1
        if n == pieces:
            place(0, n, jnp.where(taking, energies[0], energy[...]))
        else:
            place(0, n, jnp.where(taking, out0[n], own[n]))

    def step(stage, n):
        lower(stage, n).wait()
        taking = flags[order[stage]] == 1
        if n == pieces:
            place(stage + 1, n, jnp.where(taking, arrived_e[stage], held_e[stage]))
        else:
            place(stage + 1, n, jnp.where(taking, arrived[stage, n], held[stage, n]))

    sequence = [pieces] + list(range(pieces))
    ahead = 3
    for n in sequence[:ahead]:
        top(n).start()
    for tick in range(len(sequence) + stages):
        if tick < len(sequence):
            enter(sequence[tick])
            if tick + ahead < len(sequence):
                top(sequence[tick + ahead]).start()
        for stage in range(stages):
            place_in = tick - 1 - stage
            if 0 <= place_in < len(sequence):
                step(stage, sequence[place_in])


def exchange(flags, own, energy):
    bits = flags.shape[0]
    rows, wide = own.shape
    piece = rows // PIECES
    block = (PIECES, piece, wide)
    vmem = pl.BlockSpec(memory_space=pltpu.VMEM)
    tile = (8, 128)
    out0, out1, energies = pl.pallas_call(
        functools.partial(exchange_kernel, bits, PIECES),
        out_shape=[
            jax.ShapeDtypeStruct(block, own.dtype),
            jax.ShapeDtypeStruct(block, own.dtype),
            jax.ShapeDtypeStruct((ROUNDS,) + tile, jnp.float32),
        ],
        in_specs=[pl.BlockSpec(memory_space=pltpu.SMEM), vmem, vmem],
        out_specs=[vmem, vmem, vmem],
        scratch_shapes=[
            pltpu.VMEM((bits - 1,) + block, own.dtype),
            pltpu.VMEM((bits - 1,) + block, own.dtype),
            pltpu.VMEM((bits - 1,) + tile, jnp.float32),
            pltpu.VMEM((bits - 1,) + tile, jnp.float32),
            pltpu.SemaphoreType.DMA((PIECES + 1,)),
            pltpu.SemaphoreType.DMA((PIECES + 1,)),
            pltpu.SemaphoreType.DMA((bits - 1, PIECES + 1)),
            pltpu.SemaphoreType.DMA((bits - 1, PIECES + 1)),
        ],
        compiler_params=pltpu.CompilerParams(
            collective_id=1, has_side_effects=True, vmem_limit_bytes=48 * 2**20
        ),
    )(flags, own.reshape(block), jnp.broadcast_to(energy, tile))
    return (
        out0.reshape(rows, wide),
        out1.reshape(rows, wide),
        energies[0, 0, 0],
        energies[1, 0, 0],
    )


def body(ri_factors, occ_energy, vir_energy, partner, pair_weight):
    own = ri_factors[0]
    devices = lax.axis_size(AXIS)
    bits = devices.bit_length() - 1
    me = lax.axis_index(AXIS)
    rows = own.shape[1] // devices
    mask = jnp.bitwise_xor(partner[1, 0], me)
    flags = jnp.right_shift(mask, jnp.arange(bits, dtype=jnp.int32)) & 1

    fetched0, fetched1, energy0, energy1 = exchange(flags, own, occ_energy)
    fetched, energies = [fetched0, fetched1], [energy0, energy1]
    parts = []
    for turn in range(ROUNDS):
        coulomb = lax.dot_general(
            own, fetched[turn], (((1,), (1,)), ((), ())), preferred_element_type=jnp.float32
        )
        denominator = occ_energy[0] + energies[turn] - vir_energy[:, None] - vir_energy[None, :]
        amplitudes = coulomb / denominator
        combined = (2.0 * amplitudes - amplitudes.T).astype(jnp.bfloat16)
        weight = pair_weight[turn, 0].astype(jnp.float32)
        parts.append(
            (weight * jnp.dot(combined, fetched[turn], preferred_element_type=jnp.float32)).astype(
                jnp.bfloat16
            )
        )
    partial = sum(
        lax.dot_general(p, own, (((0,), (0,)), ((), ())), preferred_element_type=jnp.float32)
        for p in parts
    )
    density = density_scatter(partial.reshape(devices, rows, own.shape[1]))
    response = parts[0].astype(jnp.float32) + parts[1].astype(jnp.float32)
    return (response[None], density / float(devices))


def solution(mesh):
    placed = (P("occ", None, None), P("occ"), P(), P(None, "occ"), P(None, "occ"))
    return jax.shard_map(
        body,
        mesh=mesh,
        in_specs=placed,
        out_specs=(P("occ", None, None), P("occ", None)),
        check_vma=False,
    )
```

time: 376 us -> 175 us (0.47)
  waiting for transfers between devices: 268 us -> 0 us
  Pallas kernels: 0 us -> 136 us
  blocking collectives: 42 us -> 0 us
  between operations: 18.6 us -> 4.64 us
  local copies, waits for them, and re-layouts: 15.2 us -> 10.7 us
    ppermute x3 -> x0, waiting for transfers between devices: 137 us -> none  [from_partner(): return lax.ppermute(value, axis, pairs)]
    pallas_call x0 -> x2, Pallas kernels: none -> 136 us  [the longest x1 101 us: exchange(): pl.pallas_call(functools.partial(exchange_kernel, bits, PIECES), out_shap...]
    reduce_scatter x1 -> x0, waiting for transfers between devices: 132 us -> none  [body(): lax.psum_scatter(density_rows((response_part,), own_block, share_rows * l...]
    unnamed x1 -> x0, blocking collectives: 42 us -> none
    cond x5 -> x0, local copies, waits for them, and re-layouts: 7.25 us -> none
  transfers between devices with their start and end apart: 4 -> 0, of which waited for: 4 -> 0; matrix products, arithmetic and copies ran while one was open for 1% -> 0% of each run, Pallas kernels for 0% -> 0%
where the time goes in v1:
time: 175 us; the launch traced here: 174 us
  Pallas kernels  136 us (78%)
  matrix products  19.1 us (11%)
  local copies, waits for them, and re-layouts  10.7 us (6%)
  between operations  4.64 us (3%)
  other arithmetic  3.82 us (2%)
    pallas_call x1, Pallas kernels, exchange(): pl.pallas_call(functools.partial(exchange_kernel, bits, PIECES), out_shap...  101 us
    pallas_call x1, Pallas kernels, density_scatter(): pl.pallas_call(functools.partial(scatter_kernel, bits, orders, width), ou...  34.7 us
    dot_general x2, matrix products, body(): lax.dot_general(p, own, (((0,), (0,)), ((), ())), preferred_element_type=...  7.98 us
    dot_general x2, matrix products, body(): jnp.dot(combined, fetched[turn], preferred_element_type=jnp.float32)  7.08 us
    dot_general x2, local copies, waits for them, and re-layouts, body(): lax.dot_general(own, fetched[turn], (((1,), (1,)), ((), ())), preferred_e...  5.09 us
    dot_general x2, matrix products, body(): lax.dot_general(own, fetched[turn], (((1,), (1,)), ((), ())), preferred_e...  3.99 us

profile of v1, /device:TPU:0, one launch (start us, length us, event | category | flops | bytes accessed | tf_op | source)
XLA Modules:
  0.0 174.4 jit_solution(6485216022331494621)
XLA Ops:
  0.6 0.0 copy-start.5
  1.3 1.2 slice.16
  3.2 1.3 fusion.30
  5.8 0.0 copy-start
  5.8 1.4 copy-done
  7.2 0.0 copy-start.1
  7.2 101.5 %shard_map.71 = (bf16[8,64,1536]{2,1,0:T(8,128)(2,1)S(1)}, bf16[8,64,1536]{2,1,0:T(8,128)(2,1)S(1)}, f32[2,8,128]{2,1,0:T(8,128)S(1)}) custom-call(s32[5]{0:T(128)S(1)} %shift-right-arithmetic_and_fusion.refs_0_, bf16[8,64,1536]{2,1,0:T(8,128)(2,1)S(1)} %bitcast.48, f32[8,128]{1,0:T(8,128)S(1)} %broadcast_in_dim.4.refs_2_), custom_call_target="tpu_custom_call" | custom-call | tf_op jit(solution)/shard_map/pallas_call | solution.py:229
  108.7 0.0 copy-start.2
  108.7 1.1 copy-done.2
  109.9 0.5 fusion.29
  111.7 0.0 copy-done.5
  111.7 0.0 copy-done.1
  111.7 0.0 copy-start.3
  111.7 2.0 %fusion.7 = f32[512,512]{1,0:T(8,128)} fusion(bf16[512,1536]{1,0:T(8,128)(2,1)S(1)} %bitcast.49, bf16[1,512,1536]{2,1,0:T(8,128)(2,1)S(1)} %copy-done.1), kind=kOutput, calls=%fused_computation.11 | convolution fusion | flops 805306368 | bytes 4194304 | tf_op jit(solution)/shard_map/dot_general | solution.py:273
  113.7 0.0 copy-done.3
  113.7 2.0 %fusion.5 = f32[512,512]{1,0:T(8,128)} fusion(bf16[512,1536]{1,0:T(8,128)(2,1)S(1)} %bitcast.52, bf16[1,512,1536]{2,1,0:T(8,128)(2,1)S(1)} %copy-done.1), kind=kOutput, calls=%fused_computation.9 | convolution fusion | flops 805306368 | bytes 4194304 | tf_op jit(solution)/shard_map/dot_general | solution.py:273
  115.7 2.6 %copy.8 = f32[512,512]{0,1:T(8,128)} copy(f32[512,512]{1,0:T(8,128)} %fusion.5) | data formatting | bytes 2097152 | tf_op jit(solution)/shard_map/dot_general | solution.py:273
  118.3 4.3 %fusion.1 = bf16[512,1536]{1,0:T(8,128)(2,1)} fusion(bf16[512,1536]{1,0:T(8,128)(2,1)} %bitcast.51, f32[]{:T(128)} %bitcast.8, f32[512,512]{0,1:T(8,128)} %copy.8, f32[512,512]{1,0:T(8,128)} %fusion.5, f32[512]{0:T(512)S(1)} %get-tuple-element.11, f32[512]{0:T(512)S(1)} %copy-done.5), kind=kOutput, calls=%fused_computation.5 | convolution fusion | flops 808714240 | bytes 5246980 | tf_op jit(solution)/shard_map/dot_general | solution.py:281
  122.6 2.5 %copy.7 = f32[512,512]{0,1:T(8,128)} copy(f32[512,512]{1,0:T(8,128)} %fusion.7) | data formatting | bytes 2097152 | tf_op jit(solution)/shard_map/dot_general | solution.py:273
  125.1 0.0 copy-start.4
  125.1 2.8 %fusion = bf16[512,1536]{1,0:T(8,128)(2,1)S(1)} fusion(bf16[512,1536]{1,0:T(8,128)(2,1)S(1)} %bitcast.50, f32[]{:T(128)} %bitcast, f32[512,512]{0,1:T(8,128)} %copy.7, f32[512,512]{1,0:T(8,128)} %fusion.7, f32[512]{0:T(512)S(1)} %copy-done.5, f32[512]{0:T(512)S(1)} %get-tuple-element.10), kind=kOutput, calls=%fused_computation.4 | convolution fusion | flops 808714240 | bytes 5246980 | tf_op jit(solution)/shard_map/dot_general | solution.py:281
  127.9 0.0 copy-done.4
  127.9 2.1 %add_bitcast_fusion = f32[1,512,1536]{2,1,0:T(8,128)} fusion(bf16[512,1536]{1,0:T(8,128)(2,1)S(1)} %copy-done.4, bf16[512,1536]{1,0:T(8,128)(2,1)S(1)} %fusion), kind=kLoop, calls=%fused_computation.3 | loop fusion | flops 2359296 | bytes 6291456 | tf_op jit(solution)/shard_map/broadcast_in_dim | solution.py:291
  130.0 2.7 %fusion.3 = f32[1536,1536]{1,0:T(8,128)S(1)} fusion(bf16[512,1536]{1,0:T(8,128)(2,1)S(1)} %fusion, bf16[1,512,1536]{2,1,0:T(8,128)(2,1)S(1)} %copy-done.1), kind=kOutput, calls=%fused_computation.7 | convolution fusion | flops 2415919104 | bytes 12582912 | tf_op jit(solution)/shard_map/dot_general | solution.py:286
  132.7 5.3 %convolution_add_fusion = f32[1536,1536]{1,0:T(8,128)} fusion(f32[1536,1536]{1,0:T(8,128)S(1)} %fusion.3, bf16[512,1536]{1,0:T(8,128)(2,1)S(1)} %copy-done.4, bf16[1,512,1536]{2,1,0:T(8,128)(2,1)S(1)} %copy-done.1), kind=kOutput, calls=%fused_computation | convolution fusion | flops 2418278400 | bytes 22020096 | tf_op jit(solution)/shard_map/dot_general | solution.py:286
  138.0 34.7 %shard_map.72 = f32[48,1536]{1,0:T(8,128)} custom-call(f32[32,48,1536]{2,1,0:T(8,128)} %bitcast.53), custom_call_target="tpu_custom_call" | custom-call | tf_op jit(solution)/shard_map/pallas_call | solution.py:120
  172.7 1.7 broadcast_multiply_fusion
  (3 shorter events, 0.0 us)
Async XLA Ops:
  0.6 111.1 %copy-start.5 = (f32[512]{0:T(512)S(1)}, f32[512]{0:T(512)}, u32[]{:S(2)}) copy-start(f32[512]{0:T(512)} %param.7) | copy-start | bytes 6148
  5.8 1.4 copy-start
  7.2 104.5 %copy-start.1 = (bf16[1,512,1536]{2,1,0:T(8,128)(2,1)S(1)}, bf16[1,512,1536]{2,1,0:T(8,128)(2,1)}, u32[]{:S(2)}) copy-start(bf16[1,512,1536]{2,1,0:T(8,128)(2,1)} %param.5) | copy-start | bytes 4718596
  108.7 1.1 copy-start.2
  111.7 2.0 %copy-start.3 = (bf16[8,64,1536]{2,1,0:T(8,128)(2,1)S(1)}, bf16[8,64,1536]{2,1,0:T(8,128)(2,1)}, u32[]{:S(2)}) copy-start(bf16[8,64,1536]{2,1,0:T(8,128)(2,1)} %copy-done.2) | copy-start | bytes 4718596
  125.1 2.8 %copy-start.4 = (bf16[512,1536]{1,0:T(8,128)(2,1)S(1)}, bf16[512,1536]{1,0:T(8,128)(2,1)}, u32[]{:S(2)}) copy-start(bf16[512,1536]{1,0:T(8,128)(2,1)} %fusion.1) | copy-start | bytes 4718596

commit v2 on v1

--- a/solution.py
+++ b/solution.py
@@ -10,7 +10,9 @@
 ROUNDS = 2
 AXIS = "occ"
 CHAINS = 3
-PIECES = 8
+PIECES = 16
+GROUPS = 4
+AHEAD = 6
 
 
 def chain_orders(bits):
@@ -32,11 +34,35 @@
 
 
 def scatter_kernel(bits, orders, width, *refs):
-    part_ref, out_ref, acc = refs[0], refs[1], refs[2]
-    sends = refs[3 : 3 + bits]
-    recvs = refs[3 + bits : 3 + 2 * bits]
-    send_sem, recv_sem = refs[3 + 2 * bits], refs[4 + 2 * bits]
+    inputs, refs = refs[: -4 - 2 * bits], refs[-4 - 2 * bits :]
+    out_ref, acc = refs[0], refs[1]
+    sends = refs[2 : 2 + bits]
+    recvs = refs[2 + bits : 2 + 2 * bits]
+    send_sem, recv_sem = refs[2 + 2 * bits], refs[3 + 2 * bits]
+    fused = len(inputs) == 2
+    part_ref = acc if fused else inputs[0]
     me = lax.axis_index(AXIS)
+
+    def density_columns(chain):
+        turned_ref, own_ref = inputs
+        _, rows, _ = acc.shape
+        columns = pl.ds(chain * width, width)
+
+        def tile(t, _):
+            spot = pl.ds(pl.multiple_of(t * 8 * rows, 8 * rows), 8 * rows)
+            value = jnp.dot(
+                turned_ref[0, spot, :], own_ref[:, columns], preferred_element_type=jnp.float32
+            )
+            for turn in range(1, ROUNDS):
+                value += jnp.dot(
+                    turned_ref[turn, spot, :],
+                    own_ref[:, columns],
+                    preferred_element_type=jnp.float32,
+                )
+            acc[pl.ds(t * 8, 8), :, columns] = value.reshape(8, rows, width)
+            return 0
+
+        lax.fori_loop(0, acc.shape[0] // 8, tile, 0)
 
     def peer(bit):
         own = (me // 2**bit) % 2
@@ -96,6 +122,8 @@
         lax.fori_loop(0, count, keep_one, 0)
 
     for chain in range(CHAINS):
+        if fused:
+            density_columns(chain)
         advance(0, chain)
     for stage in range(1, bits):
         for chain in range(CHAINS):
@@ -108,8 +136,17 @@
         out_ref[:, columns] = last + recvs[bits - 1][chain, 0].astype(jnp.float32)
 
 
-def density_scatter(partial):
-    devices, rows, wide = partial.shape
+def density_scatter(turned, own):
+    devices, wide = lax.axis_size(AXIS), own.shape[1]
+    rows = wide // devices
+    if rows % 16 == 0 and devices % 8 == 0:
+        inputs = (turned, own)
+    else:
+        partial = sum(
+            jnp.dot(turned[turn], own, preferred_element_type=jnp.float32)
+            for turn in range(ROUNDS)
+        )
+        inputs = (partial.reshape(devices, rows, wide),)
     bits = devices.bit_length() - 1
     width = wide // CHAINS
     orders = chain_orders(bits)
@@ -120,7 +157,7 @@
     return pl.pallas_call(
         functools.partial(scatter_kernel, bits, orders, width),
         out_shape=jax.ShapeDtypeStruct((rows, wide), jnp.float32),
-        in_specs=[pl.BlockSpec(memory_space=pltpu.VMEM)],
+        in_specs=[pl.BlockSpec(memory_space=pltpu.VMEM)] * len(inputs),
         out_specs=pl.BlockSpec(memory_space=pltpu.VMEM),
         scratch_shapes=[pltpu.VMEM((devices, rows, wide), jnp.float32)]
         + slots
@@ -129,16 +166,23 @@
         compiler_params=pltpu.CompilerParams(
             collective_id=0, has_side_effects=True, vmem_limit_bytes=58 * 2**20
         ),
-    )(partial)
-
-
-def exchange_kernel(bits, pieces, *refs):
-    flags, own, energy, out0, out1, energies = refs[:6]
+    )(*inputs)
+
+
+def exchange_kernel(bits, *refs):
+    flags, weights, own, energy, vir_row, vir_col, parts, turned = refs[:8]
+    out0, out1, energies, coulomb, held, arrived, held_e, arrived_e = refs[8:16]
+    top_send, top_recv, low_send, low_recv = refs[16:20]
     stages = bits - 1
-    held, arrived, held_e, arrived_e = refs[6:10]
-    top_send, top_recv, low_send, low_recv = refs[10:14]
+    rows, wide = own.shape
+    piece = rows // PIECES
+    group = PIECES // GROUPS
     me = lax.axis_index(AXIS)
     order = list(range(stages - 1, -1, -1))
+    blocks = [out0, out1]
+
+    def span(n, count=1):
+        return pl.ds(n * piece, count * piece)
 
     def peer(bit):
         mine = (me // 2**bit) % 2
@@ -162,82 +206,122 @@
         )
 
     def top(n):
-        if n == pieces:
+        if n == PIECES:
             src, dst = energy, energies.at[0]
         else:
-            src, dst = own.at[n], out0.at[n]
+            src, dst = own.at[span(n)], out0.at[span(n)]
         return remote(src, dst, top_send.at[n], top_recv.at[n], bits - 1)
 
     def lower(stage, n):
-        if n == pieces:
+        if n == PIECES:
             src, dst = held_e.at[stage], arrived_e.at[stage]
         else:
-            src, dst = held.at[stage, n], arrived.at[stage, n]
+            src, dst = held.at[stage, span(n)], arrived.at[stage, span(n)]
         return remote(src, dst, low_send.at[stage, n], low_recv.at[stage, n], order[stage])
 
     def place(stage, n, value):
-        if n == pieces:
+        if n == PIECES:
             if stage == stages:
                 energies[1] = value
             else:
                 held_e[stage] = value
         elif stage == stages:
-            out1[n] = value
-        else:
-            held[stage, n] = value
+            out1[span(n)] = value
+        else:
+            held[stage, span(n)] = value
         if stage < stages:
             lower(stage, n).start()
 
     def enter(n):
         top(n).wait()
         taking = flags[bits - 1] == 1
-        if n == pieces:
+        if n == PIECES:
             place(0, n, jnp.where(taking, energies[0], energy[...]))
         else:
-            place(0, n, jnp.where(taking, out0[n], own[n]))
+            place(0, n, jnp.where(taking, out0[span(n)], own[span(n)]))
 
     def step(stage, n):
         lower(stage, n).wait()
         taking = flags[order[stage]] == 1
-        if n == pieces:
+        if n == PIECES:
             place(stage + 1, n, jnp.where(taking, arrived_e[stage], held_e[stage]))
         else:
-            place(stage + 1, n, jnp.where(taking, arrived[stage, n], held[stage, n]))
-
-    sequence = [pieces] + list(range(pieces))
-    ahead = 3
-    for n in sequence[:ahead]:
+            place(
+                stage + 1, n, jnp.where(taking, arrived[stage, span(n)], held[stage, span(n)])
+            )
+
+    def coulomb_rows(turn, n):
+        if n == PIECES or (n + 1) % group:
+            return
+        spot = span(n + 1 - group, group)
+        coulomb[turn, spot, :] = lax.dot_general(
+            blocks[turn][spot, :],
+            own[...],
+            (((1,), (1,)), ((), ())),
+            preferred_element_type=jnp.float32,
+        )
+
+    def finish(turn):
+        both = energy[0:1, 0:1] + energies[turn, 0:1, 0:1]
+        flipped = coulomb[turn] / (both - vir_row[...] - vir_col[...])
+        combined = (2.0 * flipped.T - flipped).astype(jnp.bfloat16)
+        weight = weights[turn]
+        width = wide // CHAINS
+
+        def tile(t, _):
+            spot = pl.ds(pl.multiple_of(t * width, width), width)
+            product = jnp.dot(
+                combined, blocks[turn][:, spot], preferred_element_type=jnp.float32
+            )
+            part = (weight * product).astype(jnp.bfloat16)
+            parts[turn, :, spot] = part
+            turned[turn, spot, :] = part.T
+            return 0
+
+        lax.fori_loop(0, CHAINS, tile, 0)
+
+    sequence = [PIECES] + list(range(PIECES))
+    for n in sequence[:AHEAD]:
         top(n).start()
     for tick in range(len(sequence) + stages):
         if tick < len(sequence):
             enter(sequence[tick])
-            if tick + ahead < len(sequence):
-                top(sequence[tick + ahead]).start()
+            if tick + AHEAD < len(sequence):
+                top(sequence[tick + AHEAD]).start()
         for stage in range(stages):
             place_in = tick - 1 - stage
             if 0 <= place_in < len(sequence):
                 step(stage, sequence[place_in])
-
-
-def exchange(flags, own, energy):
+        if tick < len(sequence):
+            coulomb_rows(0, sequence[tick])
+        if tick == len(sequence):
+            finish(0)
+        if tick >= stages:
+            coulomb_rows(1, sequence[tick - stages])
+    finish(1)
+
+
+def exchange(flags, weights, own, energy, vir_energy):
     bits = flags.shape[0]
     rows, wide = own.shape
-    piece = rows // PIECES
-    block = (PIECES, piece, wide)
+    smem = pl.BlockSpec(memory_space=pltpu.SMEM)
     vmem = pl.BlockSpec(memory_space=pltpu.VMEM)
     tile = (8, 128)
-    out0, out1, energies = pl.pallas_call(
-        functools.partial(exchange_kernel, bits, PIECES),
+    return pl.pallas_call(
+        functools.partial(exchange_kernel, bits),
         out_shape=[
-            jax.ShapeDtypeStruct(block, own.dtype),
-            jax.ShapeDtypeStruct(block, own.dtype),
-            jax.ShapeDtypeStruct((ROUNDS,) + tile, jnp.float32),
+            jax.ShapeDtypeStruct((ROUNDS, rows, wide), own.dtype),
+            jax.ShapeDtypeStruct((ROUNDS, wide, rows), own.dtype),
         ],
-        in_specs=[pl.BlockSpec(memory_space=pltpu.SMEM), vmem, vmem],
-        out_specs=[vmem, vmem, vmem],
+        in_specs=[smem, smem, vmem, vmem, vmem, vmem],
+        out_specs=[vmem, vmem],
         scratch_shapes=[
-            pltpu.VMEM((bits - 1,) + block, own.dtype),
-            pltpu.VMEM((bits - 1,) + block, own.dtype),
+            pltpu.VMEM((rows, wide), own.dtype),
+            pltpu.VMEM((rows, wide), own.dtype),
+            pltpu.VMEM((ROUNDS,) + tile, jnp.float32),
+            pltpu.VMEM((ROUNDS, rows, rows), jnp.float32),
+            pltpu.VMEM((bits - 1, rows, wide), own.dtype),
+            pltpu.VMEM((bits - 1, rows, wide), own.dtype),
             pltpu.VMEM((bits - 1,) + tile, jnp.float32),
             pltpu.VMEM((bits - 1,) + tile, jnp.float32),
             pltpu.SemaphoreType.DMA((PIECES + 1,)),
@@ -246,14 +330,15 @@
             pltpu.SemaphoreType.DMA((bits - 1, PIECES + 1)),
         ],
         compiler_params=pltpu.CompilerParams(
-            collective_id=1, has_side_effects=True, vmem_limit_bytes=48 * 2**20
+            collective_id=1, has_side_effects=True, vmem_limit_bytes=56 * 2**20
         ),
-    )(flags, own.reshape(block), jnp.broadcast_to(energy, tile))
-    return (
-        out0.reshape(rows, wide),
-        out1.reshape(rows, wide),
-        energies[0, 0, 0],
-        energies[1, 0, 0],
+    )(
+        flags,
+        weights,
+        own,
+        jnp.broadcast_to(energy, tile),
+        vir_energy.reshape(1, rows),
+        vir_energy.reshape(rows, 1),
     )
 
 
@@ -262,31 +347,11 @@
     devices = lax.axis_size(AXIS)
     bits = devices.bit_length() - 1
     me = lax.axis_index(AXIS)
-    rows = own.shape[1] // devices
     mask = jnp.bitwise_xor(partner[1, 0], me)
     flags = jnp.right_shift(mask, jnp.arange(bits, dtype=jnp.int32)) & 1
-
-    fetched0, fetched1, energy0, energy1 = exchange(flags, own, occ_energy)
-    fetched, energies = [fetched0, fetched1], [energy0, energy1]
-    parts = []
-    for turn in range(ROUNDS):
-        coulomb = lax.dot_general(
-            own, fetched[turn], (((1,), (1,)), ((), ())), preferred_element_type=jnp.float32
-        )
-        denominator = occ_energy[0] + energies[turn] - vir_energy[:, None] - vir_energy[None, :]
-        amplitudes = coulomb / denominator
-        combined = (2.0 * amplitudes - amplitudes.T).astype(jnp.bfloat16)
-        weight = pair_weight[turn, 0].astype(jnp.float32)
-        parts.append(
-            (weight * jnp.dot(combined, fetched[turn], preferred_element_type=jnp.float32)).astype(
-                jnp.bfloat16
-            )
-        )
-    partial = sum(
-        lax.dot_general(p, own, (((0,), (0,)), ((), ())), preferred_element_type=jnp.float32)
-        for p in parts
-    )
-    density = density_scatter(partial.reshape(devices, rows, own.shape[1]))
+    weights = pair_weight[:, 0].astype(jnp.float32)
+    parts, turned = exchange(flags, weights, own, occ_energy, vir_energy)
+    density = density_scatter(turned, own)
     response = parts[0].astype(jnp.float32) + parts[1].astype(jnp.float32)
     return (response[None], density / float(devices))
 

time: 175 us -> 159 us (0.909)
  matrix products: 19.1 us -> 0 us
  Pallas kernels: 136 us -> 148 us
  local copies, waits for them, and re-layouts: 10.7 us -> 3.4 us
  between operations: 4.64 us -> 1.95 us
  other arithmetic: 3.82 us -> 5.58 us
    dot_general x6 -> x0, matrix products: 19.1 us -> none  [the longest x2 7.98 us: body(): lax.dot_general(p, own, (((0,), (0,)), ((), ())), preferred_element_type=...]
    pallas_call x1, Pallas kernels: 34.7 us -> 42.4 us  [density_scatter(): pl.pallas_call(functools.partial(scatter_kernel, bits, orders, width), ou...]
    dot_general x2 -> x0, local copies, waits for them, and re-layouts: 5.09 us -> none  [body(): lax.dot_general(own, fetched[turn], (((1,), (1,)), ((), ())), preferred_e...]
    pallas_call x1, Pallas kernels: 101 us -> 105 us  [exchange(): pl.pallas_call(functools.partial(exchange_kernel, bits), out_shape=[jax.S...]
    unnamed x12 -> x2, local copies, waits for them, and re-layouts: 2.56 us -> 0.01 us
    add x0 -> x1, other arithmetic: none -> 2.11 us  [body(): response = parts[0].astype(jnp.float32) + parts[1].astype(jnp.float32)]
    broadcast_in_dim x1 -> x0, other arithmetic: 2.11 us -> none  [body(): return (response[None], density / float(devices))]
    slice x2 -> x0, local copies, waits for them, and re-layouts: 1.85 us -> none  [the longest x1 1.31 us: body(): weight = pair_weight[turn, 0].astype(jnp.float32)]
where the time goes in v2:
time: 159 us
  Pallas kernels  148 us (93%)
  other arithmetic  5.58 us (4%)
  local copies, waits for them, and re-layouts  3.4 us (2%)
  between operations  1.95 us (1%)
    pallas_call x1, Pallas kernels, exchange(): pl.pallas_call(functools.partial(exchange_kernel, bits), out_shape=[jax.S...  105 us
    pallas_call x1, Pallas kernels, density_scatter(): pl.pallas_call(functools.partial(scatter_kernel, bits, orders, width), ou...  42.4 us

profile of v2, /device:TPU:0, one launch (start us, length us, event | category | flops | bytes accessed | tf_op | source)
XLA Modules:
  0.0 158.7 jit_solution(2449779532887461287)
XLA Ops:
  0.6 1.5 copy.7.refs_5_
  2.8 0.6 broadcast_in_dim.2.refs_3_
  3.4 1.3 slice.9
  5.3 0.6 shift-right-arithmetic_and_fusion.refs_0_
  5.9 1.2 convert_bitcast_fusion.refs_1_
  7.1 105.4 %shard_map.71 = (bf16[2,512,1536]{2,1,0:T(8,128)(2,1)}, bf16[2,1536,512]{2,1,0:T(8,128)(2,1)}) custom-call(s32[5]{0:T(128)} %shift-right-arithmetic_and_fusion.refs_0_, f32[2]{0:T(128)} %convert_bitcast_fusion.refs_1_, bf16[512,1536]{1,0:T(8,128)(2,1)} %bitcast.8, f32[8,128]{1,0:T(8,128)} %broadcast_in_dim.2.refs_3_, f32[1,512]{1,0:T(1,128)} %bitcast.11, ...), custom_call_target="tpu_custom_call" | custom-call | tf_op jit(solution)/shard_map/pallas_call | solution.py:310
  112.5 0.0 copy-start
  112.5 42.4 %shard_map.72 = f32[48,1536]{1,0:T(8,128)} custom-call(bf16[2,1536,512]{2,1,0:T(8,128)(2,1)} %get-tuple-element.5.refs_0_, bf16[512,1536]{1,0:T(8,128)(2,1)} %bitcast.9), custom_call_target="tpu_custom_call" | custom-call | tf_op jit(solution)/shard_map/pallas_call | solution.py:157
  154.9 1.7 %broadcast_multiply_fusion = f32[48,1536]{1,0:T(8,128)} fusion(f32[48,1536]{1,0:T(8,128)} %shard_map.72), kind=kLoop, calls=%fused_computation.1 | loop fusion | flops 73728 | bytes 589824 | tf_op jit(solution)/shard_map/div | solution.py:356
  156.6 0.0 copy-done
  156.6 2.1 %convert_add_fusion = f32[1,512,1536]{2,1,0:T(8,128)} fusion(bf16[2,512,1536]{2,1,0:T(8,128)(2,1)S(1)} %copy-done), kind=kLoop, calls=%fused_computation | loop fusion | flops 2359296 | bytes 6291456 | tf_op jit(solution)/shard_map/add | solution.py:355
Async XLA Ops:
  112.5 44.1 %copy-start = (bf16[2,512,1536]{2,1,0:T(8,128)(2,1)S(1)}, bf16[2,512,1536]{2,1,0:T(8,128)(2,1)}, u32[]{:S(2)}) copy-start(bf16[2,512,1536]{2,1,0:T(8,128)(2,1)} %get-tuple-element.4) | copy-start | bytes 9437188
